TPU v7x, 256 devices: a whole 4x4x8 slice. The times are simulated.
256 devices in a mesh: tm: 8 (over x, z_lo), row: 4 (over z_hi), head: 8 (over y, core).
Axes of the slice: x: 4, y: 4, z: 8 (z_hi: 4, z_lo: 2; z = z_hi * 2 + z_lo), core: 2. Of those that a mesh axis runs over, the one named last changes fastest.
Arguments:
- query: bfloat16 [8, 4, 2, 384, 3072], P('tm', 'row', None, None, 'head'), may hold values from -8 to 8
- key_tiles: bfloat16 [8, 4, 2, 384, 3072], P('tm', 'row', None, None, 'head'), may hold values from -8 to 8
- value_tiles: bfloat16 [8, 4, 2, 384, 3072], P('tm', 'row', None, None, 'head'), may hold values from -6 to 6
- grad_out: bfloat16 [8, 4, 2, 384, 3072], P('tm', 'row', None, None, 'head'), may hold values from -24 to 24
- neighbours: int32 [8, 4, 2, 8], P('tm', 'row'), may hold values from -1 to 17, as said below
Outputs:
- grad_query: bfloat16 [8, 4, 2, 384, 3072], P('tm', 'row', None, None, 'head')
- grad_key: bfloat16 [8, 4, 2, 384, 3072], P('tm', 'row', None, None, 'head')
- grad_value: bfloat16 [8, 4, 2, 384, 3072], P('tm', 'row', None, None, 'head')
Inputs may be any that keep to these rules, and one draw needn't show every extreme that they name: `neighbours`: entry n of a tile's list at time block t and row block r is (3 * (dt + 1) + (dr + 1)) * 2 + j with dt, dr in -1, 0, 1 such that time block t + dt and row block r + dr exist; entry 0 names the tile itself; the named values of one list are distinct; entries equal to -1 are unused and stand after all used ones; the number of used entries is the smaller of 8 and 2 times the number of existing blocks among the nine around (t, r).
All inputs are finite; a program needn't handle non-finite values.
Results may differ from a plain program's by a relative error of at most 0.0078.
Values may be sent and summed in bfloat16 or wider, within the bound.
A program may use at most 128 MiB of HBM per device.

v0:
```python
from functools import partial

import jax
import jax.numpy as jnp
from jax import lax
from jax.sharding import PartitionSpec as P

HD = 128


def from_behind(value, axis, steps):
    count = lax.axis_size(axis)
    initial, last = (max(0, -steps), min(count, count - steps))
    return lax.ppermute(value, axis, [(source, source + steps) for source in range(initial, last)])


def padded_2(block, sides, width):
    for axis, dim in sides:
        count = lax.axis_size(axis)
        forward = [(i, i + 1) for i in range(count - 1)]
        backward = [(target, source) for source, target in forward]
        low = lax.ppermute(
            lax.slice_in_dim(block, block.shape[dim] - width, None, axis=dim), axis, forward
        )
        high = lax.ppermute(lax.slice_in_dim(block, 0, width, axis=dim), axis, backward)
        block = jnp.concatenate([low, block, high], axis=dim)
    return block


def tile_backward(running, inputs, key_head, value_head, score_scale):
    query_tile, grad_tile, entries = inputs
    is_live = entries >= 0
    picked = jnp.maximum(entries, 0)
    keys_used = key_head[picked]
    values_used = value_head[picked]
    scores = (
        jnp.einsum("qd,nkd->qnk", query_tile, keys_used, preferred_element_type=jnp.float32)
        * score_scale
    )
    scores = jnp.where(is_live[None, :, None], scores, -1e30)
    row_peak = jnp.max(scores, axis=(1, 2), keepdims=True)
    log_total = row_peak + jnp.log(jnp.sum(jnp.exp(scores - row_peak), axis=(1, 2), keepdims=True))
    attn_probs = jnp.exp(scores - log_total)
    grad_probs = jnp.einsum(
        "qd,nkd->qnk", grad_tile, values_used, preferred_element_type=jnp.float32
    )
    row_delta = jnp.sum(attn_probs * grad_probs, axis=(1, 2), keepdims=True)
    grad_scores = attn_probs * (grad_probs - row_delta)
    low_probs = attn_probs.astype(jnp.bfloat16)
    low_grads = grad_scores.astype(jnp.bfloat16)
    grad_query = (
        jnp.einsum("qnk,nkd->qd", low_grads, keys_used, preferred_element_type=jnp.float32)
        * score_scale
    )
    value_terms = jnp.einsum(
        "qnk,qd->nkd", low_probs, grad_tile, preferred_element_type=jnp.float32
    )
    key_terms = (
        jnp.einsum("qnk,qd->nkd", low_grads, query_tile, preferred_element_type=jnp.float32)
        * score_scale
    )
    live_mask = is_live[:, None, None]
    key_sum = running[0].at[picked].add(jnp.where(live_mask, key_terms, 0.0))
    value_sum = running[1].at[picked].add(jnp.where(live_mask, value_terms, 0.0))
    return ((key_sum, value_sum), grad_query)


def row_forward(piece, shift_by):
    return from_behind(piece, "row", shift_by)


def time_forward(piece, shift_by):
    return from_behind(piece, "tm", shift_by)


def sectioned_return(parts):
    from_below = row_forward(parts[:, 2], 1)
    from_above = row_forward(parts[:, 0], -1)
    middle = parts[:, 1]
    totals = (
        middle[1].astype(jnp.float32)
        + from_below[1].astype(jnp.float32)
        + from_above[1].astype(jnp.float32)
    )
    for time_off in (0, 2):
        bundle = jnp.stack((middle[time_off], from_below[time_off], from_above[time_off]))
        arrived = time_forward(bundle, time_off - 1)
        totals = totals + jnp.sum(arrived.astype(jnp.float32), axis=0)
    return totals


def per_device(query, key_tiles, value_tiles, grad_out, neighbours):
    tile_count = query.shape[2]
    tile_len = query.shape[3]
    channels = query.shape[4]
    slot_count = 9 * tile_count
    score_scale = HD ** (-0.5)
    stacked = jnp.stack((key_tiles, value_tiles), axis=2)
    padded = padded_2(stacked, (("tm", 0), ("row", 1)), 1)
    key_slots = padded[:, :, 0].reshape(slot_count, tile_len, channels)
    value_slots = padded[:, :, 1].reshape(slot_count, tile_len, channels)
    entry_lists = neighbours[0, 0]
    query_local = query[0, 0]
    grad_local = grad_out[0, 0]
    query_grads = []
    key_parts = []
    value_parts = []
    for head_index in range(channels // HD):
        lower = head_index * HD
        upper = lower + HD
        stepper = partial(
            tile_backward,
            key_head=key_slots[:, :, lower:upper],
            value_head=value_slots[:, :, lower:upper],
            score_scale=score_scale,
        )
        zeros = jnp.zeros((slot_count, tile_len, HD), jnp.float32)
        sums, head_grads = lax.scan(
            stepper,
            (zeros, zeros),
            (query_local[:, :, lower:upper], grad_local[:, :, lower:upper], entry_lists),
        )
        query_grads.append(head_grads)
        key_parts.append(sums[0])
        value_parts.append(sums[1])
    grad_query = jnp.concatenate(query_grads, axis=-1).astype(jnp.bfloat16)[None, None]
    key_part = jnp.concatenate(key_parts, axis=-1).reshape(3, 3, tile_count, tile_len, channels)
    value_part = jnp.concatenate(value_parts, axis=-1).reshape(3, 3, tile_count, tile_len, channels)
    parts = jnp.stack((key_part, value_part), axis=2).astype(jnp.bfloat16)
    totals = sectioned_return(parts)
    grad_key = totals[0].astype(jnp.bfloat16)[None, None]
    grad_value = totals[1].astype(jnp.bfloat16)[None, None]
    return (grad_query, grad_key, grad_value)


def solution(mesh):
    in_specs = (
        P("tm", "row", None, None, "head"),
        P("tm", "row", None, None, "head"),
        P("tm", "row", None, None, "head"),
        P("tm", "row", None, None, "head"),
        P("tm", "row", None, None),
    )
    out_specs = (
        P("tm", "row", None, None, "head"),
        P("tm", "row", None, None, "head"),
        P("tm", "row", None, None, "head"),
    )
    return jax.shard_map(
        per_device, mesh=mesh, in_specs=in_specs, out_specs=out_specs, check_vma=False
    )
```

profile of v0, /device:TPU:20, one launch (start us, length us, event | category | flops | bytes accessed | tf_op | source)
XLA Modules:
  0.0 787.8 jit_solution(12538217553441956103)
XLA Ops:
  2.0 4.0 collective-permute-start
  6.0 2.9 collective-permute-start.1
  8.9 24.9 %collective-permute-done = bf16[1,1,2,2,384,384]{5,4,3,2,1,0:T(8,128)(2,1)S(1)} collective-permute-done((bf16[1,1,2,2,384,384]{5,4,3,2,1,0:T(8,128)(2,1)S(1)}, bf16[1,1,2,2,384,384]{5,4,3,2,1,0:T(8,128)(2,1)S(1)}, u32[]{:S(2)}, u32[]{:S(2)}) %collective-permute-start) | collective-permute-done | bytes 1179680 | tf_op jit(solution)/shard_map/ppermute | solution.py:22
  33.8 23.9 %collective-permute-done.1 = bf16[1,1,2,2,384,384]{5,4,3,2,1,0:T(8,128)(2,1)S(1)} collective-permute-done((bf16[1,1,2,2,384,384]{5,4,3,2,1,0:T(8,128)(2,1)S(1)}, bf16[1,1,2,2,384,384]{5,4,3,2,1,0:T(8,128)(2,1)S(1)}, u32[]{:S(2)}, u32[]{:S(2)}) %collective-permute-start.1) | collective-permute-done | bytes 1179680 | tf_op jit(solution)/shard_map/ppermute | solution.py:25
  57.7 3.5 pad_maximum_fusion.3
  61.1 6.9 collective-permute-start.2
  69.3 2.2 fusion.105
  71.5 70.0 %collective-permute-done.2 = bf16[3,1,2,2,384,384]{5,4,3,2,1,0:T(8,128)(2,1)} collective-permute-done((bf16[3,1,2,2,384,384]{5,4,3,2,1,0:T(8,128)(2,1)}, bf16[3,1,2,2,384,384]{5,4,3,2,1,0:T(8,128)(2,1)}, u32[]{:S(2)}, u32[]{:S(2)}) %collective-permute-start.2) | collective-permute-done | bytes 3538976 | tf_op jit(solution)/shard_map/ppermute | solution.py:22
  141.5 6.9 collective-permute-done.3
  148.4 8.8 %pad_maximum_fusion = bf16[3,3,2,2,384,384]{5,4,3,2,1,0:T(8,128)(2,1)} fusion(bf16[3,1,2,2,384,384]{5,4,3,2,1,0:T(8,128)(2,1)} %collective-permute-done.3, bf16[1,1,2,2,384,384]{5,4,3,2,1,0:T(8,128)(2,1)} %copy-done.14, bf16[1,1,1,2,384,384]{5,4,3,2,1,0:T(8,128)(2,1)S(1)} %bitcast.250, bf16[1,1,1,2,384,384]{5,4,3,2,1,0:T(8,128)(2,1)S(1)} %bitcast.253, ...), kind=kLoop, calls=%fused_computation.135 | loop fusion | flops 26542080 | bytes 21233664 | tf_op jit(solution)/shard_map/concatenate | solution.py:26
  157.2 9.7 %fusion.100 = (bf16[3,3,1,2,384,384]{5,4,3,2,1,0:T(8,128)(2,1)}, bf16[3,3,1,2,384,384]{5,4,3,2,1,0:T(8,128)(2,1)}) fusion(bf16[3,3,2,2,384,384]{5,4,3,2,1,0:T(8,128)(2,1)} %pad_maximum_fusion), kind=kLoop, calls=%fused_computation.166 | loop fusion | bytes 21233664 | tf_op jit(solution)/shard_map/slice | solution.py:101
  166.9 7.8 fusion.101
  174.8 2.2 broadcast.111.clone.4
  179.8 64.5 %while.42 = (s32[]{:T(128)}, f32[18,384,128]{2,1,0:T(8,128)}, f32[18,384,128]{2,1,0:T(8,128)}, bf16[2,384,128]{2,1,0:T(8,128)(2,1)}, s32[2,8]{1,0:T(2,128)S(1)},...) while((s32[]{:T(128)}, f32[18,384,128]{2,1,0:T(8,128)}, ...), condition=%wide.region_6.7_spmd, body=%wide.region_0.6_spmd.sunk | while | flops 1537917184 | bytes 96559664 | solution.py:118
  179.8 2.2 gather_fusion
  186.0 2.2 gather_fusion.1
  188.3 3.9 multiply_reduce_fusion.6
  195.5 4.5 scatter_fusion
  200.0 4.6 fusion.164
  204.7 4.5 scatter_fusion.1
  211.8 2.2 gather_fusion
  218.1 2.2 gather_fusion.1
  220.3 3.9 multiply_reduce_fusion.6
  227.5 4.5 scatter_fusion
  232.0 4.6 fusion.164
  236.7 4.5 scatter_fusion.1
  244.3 3.6 convert.47
  247.8 2.2 broadcast.111.clone.2
  252.2 62.6 %while.43 = (s32[]{:T(128)}, f32[18,384,128]{2,1,0:T(8,128)}, f32[18,384,128]{2,1,0:T(8,128)}, bf16[2,384,128]{2,1,0:T(8,128)(2,1)S(1)}, s32[2,8]{1,0:T(2,128)S(...) while((s32[]{:T(128)}, f32[18,384,128]{2,1,0:T(8,128)}, ...), condition=%wide.region_13.14_spmd, body=%wide.region_7.13_spmd.sunk | while | flops 1537917184 | bytes 94986744 | solution.py:118
  252.2 2.2 gather_fusion.2
  258.5 2.2 gather_fusion.3
  260.7 3.9 multiply_reduce_fusion.7
  267.9 4.5 scatter_fusion.2
  272.4 4.6 fusion.175
  277.1 4.5 scatter_fusion.3
  283.6 2.2 gather_fusion.2
  289.8 2.2 gather_fusion.3
  292.1 3.9 multiply_reduce_fusion.7
  299.2 4.5 scatter_fusion.2
  303.7 4.6 fusion.175
  308.4 4.5 scatter_fusion.3
  314.9 3.7 convert.48
  318.6 2.1 broadcast.111.clone
  320.7 2.2 broadcast.111.clone.1
  323.0 62.8 %while.44 = (s32[]{:T(128)}, f32[18,384,128]{2,1,0:T(8,128)}, f32[18,384,128]{2,1,0:T(8,128)}, bf16[2,384,128]{2,1,0:T(8,128)(2,1)S(1)}, s32[2,8]{1,0:T(2,128)S(...) while((s32[]{:T(128)}, f32[18,384,128]{2,1,0:T(8,128)}, ...), condition=%wide.region_20.21_spmd, body=%wide.region_14.20_spmd.sunk | while | flops 1537917184 | bytes 94986744 | solution.py:118
  323.2 2.2 gather_fusion.4
  329.5 2.2 gather_fusion.5
  331.7 3.9 multiply_reduce_fusion.8
  338.9 4.5 scatter_fusion.4
  343.4 4.6 fusion.186
  348.0 4.5 scatter_fusion.5
  354.5 2.2 gather_fusion.4
  360.8 2.2 gather_fusion.5
  363.0 3.9 multiply_reduce_fusion.8
  370.2 4.5 scatter_fusion.4
  374.7 4.6 fusion.186
  379.3 4.5 scatter_fusion.5
  385.8 2.5 convert.49
  395.4 75.9 %collective-permute-start.4 = (bf16[3,2,2,384,384]{4,3,2,1,0:T(8,128)(2,1)S(1)}, bf16[3,2,2,384,384]{4,3,2,1,0:T(8,128)(2,1)S(1)}, u32[]{:S(2)}, u32[]{:S(2)}) collective-permute-start(bf16[3,2,2,384,384]{4,3,2,1,0:T(8,128)(2,1)S(1)} %get-tuple-element.227), channel_id=1, source_target_pairs={{0,8},{8,16},{16,24},{1,9},{9,17},{17,25},{2,10},{10,18},{18,26},{... | collective-permute-start | bytes 10616840 | tf_op jit(solution)/shard_map/ppermute | solution.py:14
  473.1 37.0 %collective-permute-done.4 = bf16[3,2,2,384,384]{4,3,2,1,0:T(8,128)(2,1)S(1)} collective-permute-done((bf16[3,2,2,384,384]{4,3,2,1,0:T(8,128)(2,1)S(1)}, bf16[3,2,2,384,384]{4,3,2,1,0:T(8,128)(2,1)S(1)}, u32[]{:S(2)}, u32[]{:S(2)}) %collective-permute-start.4) | collective-permute-done | bytes 3538976 | tf_op jit(solution)/shard_map/ppermute | solution.py:14
  510.4 81.5 %collective-permute-done.5 = bf16[3,2,2,384,384]{4,3,2,1,0:T(8,128)(2,1)S(1)} collective-permute-done((bf16[3,2,2,384,384]{4,3,2,1,0:T(8,128)(2,1)S(1)}, bf16[3,2,2,384,384]{4,3,2,1,0:T(8,128)(2,1)S(1)}, u32[]{:S(2)}, u32[]{:S(2)}) %collective-permute-start.5) | collective-permute-done | bytes 3538976 | tf_op jit(solution)/shard_map/ppermute | solution.py:14
  592.6 33.6 %collective-permute-start.6 = (bf16[3,2,2,384,384]{4,3,2,1,0:T(8,128)(2,1)S(1)}, bf16[3,2,2,384,384]{4,3,2,1,0:T(8,128)(2,1)S(1)}, u32[]{:S(2)}, u32[]{:S(2)}) collective-permute-start(bf16[3,2,2,384,384]{4,3,2,1,0:T(8,128)(2,1)S(1)} %pad_maximum_fusion.4), channel_id=1, source_target_pairs={{32,0},{64,32},{96,64},{128,96},{160,128},{192,160},{224,192},{33,... | collective-permute-start | bytes 10616840 | tf_op jit(solution)/shard_map/ppermute | solution.py:14
  629.7 73.6 %collective-permute-done.6 = bf16[3,2,2,384,384]{4,3,2,1,0:T(8,128)(2,1)S(1)} collective-permute-done((bf16[3,2,2,384,384]{4,3,2,1,0:T(8,128)(2,1)S(1)}, bf16[3,2,2,384,384]{4,3,2,1,0:T(8,128)(2,1)S(1)}, u32[]{:S(2)}, u32[]{:S(2)}) %collective-permute-start.6) | collective-permute-done | bytes 3538976 | tf_op jit(solution)/shard_map/ppermute | solution.py:14
  703.8 81.3 %collective-permute-done.7 = bf16[3,2,2,384,384]{4,3,2,1,0:T(8,128)(2,1)S(1)} collective-permute-done((bf16[3,2,2,384,384]{4,3,2,1,0:T(8,128)(2,1)S(1)}, bf16[3,2,2,384,384]{4,3,2,1,0:T(8,128)(2,1)S(1)}, u32[]{:S(2)}, u32[]{:S(2)}) %collective-permute-start.7) | collective-permute-done | bytes 3538976 | tf_op jit(solution)/shard_map/ppermute | solution.py:14
  (169 shorter events, 81.1 us)
Async XLA Ops:
  2.0 146.4 %copy-start.12 = (bf16[1,1,2,384,384]{4,3,2,1,0:T(8,128)(2,1)S(1)}, bf16[1,1,2,384,384]{4,3,2,1,0:T(8,128)(2,1)}, u32[]{:S(2)}) copy-start(bf16[1,1,2,384,384]{4,3,2,1,0:T(8,128)(2,1)} %param.13) | copy-start | bytes 1769476
  2.0 146.4 %copy-start.13 = (bf16[1,1,2,384,384]{4,3,2,1,0:T(8,128)(2,1)S(1)}, bf16[1,1,2,384,384]{4,3,2,1,0:T(8,128)(2,1)}, u32[]{:S(2)}) copy-start(bf16[1,1,2,384,384]{4,3,2,1,0:T(8,128)(2,1)} %param.12) | copy-start | bytes 1769476
  2.0 31.8 %collective-permute-start = (bf16[1,1,2,2,384,384]{5,4,3,2,1,0:T(8,128)(2,1)S(1)}, bf16[1,1,2,2,384,384]{5,4,3,2,1,0:T(8,128)(2,1)S(1)}, u32[]{:S(2)}, u32[]{:S(2)}) collective-permute-start(bf16[1,1,2,2,384,384]{5,4,3,2,1,0:T(8,128)(2,1)S(1)} %pad_maximum_fusion.7), channel_id=1, source_target_pairs={{0,32},{32,64},{64,96},{96,128},{128,160},{160,192},{192,224},{1,3... | collective-permute-start | bytes 3538952 | tf_op jit(solution)/shard_map/ppermute | solution.py:22
  6.0 51.7 %collective-permute-start.1 = (bf16[1,1,2,2,384,384]{5,4,3,2,1,0:T(8,128)(2,1)S(1)}, bf16[1,1,2,2,384,384]{5,4,3,2,1,0:T(8,128)(2,1)S(1)}, u32[]{:S(2)}, u32[]{:S(2)}) collective-permute-start(bf16[1,1,2,2,384,384]{5,4,3,2,1,0:T(8,128)(2,1)S(1)} %pad_maximum_fusion.7), channel_id=1, source_target_pairs={{32,0},{64,32},{96,64},{128,96},{160,128},{192,160},{224,192},{33,... | collective-permute-start | bytes 3538952 | tf_op jit(solution)/shard_map/ppermute | solution.py:25
  57.7 3.5 copy-start.14
  61.1 80.4 %collective-permute-start.2 = (bf16[3,1,2,2,384,384]{5,4,3,2,1,0:T(8,128)(2,1)}, bf16[3,1,2,2,384,384]{5,4,3,2,1,0:T(8,128)(2,1)}, u32[]{:S(2)}, u32[]{:S(2)}) collective-permute-start(bf16[3,1,2,2,384,384]{5,4,3,2,1,0:T(8,128)(2,1)} %pad_maximum_fusion.3), channel_id=1, source_target_pairs={{0,8},{8,16},{16,24},{1,9},{9,17},{17,25},{2,10},{10,18},{18,26},{... | collective-permute-start | bytes 10616840 | tf_op jit(solution)/shard_map/ppermute | solution.py:22
  68.1 80.3 %collective-permute-start.3 = (bf16[3,1,2,2,384,384]{5,4,3,2,1,0:T(8,128)(2,1)}, bf16[3,1,2,2,384,384]{5,4,3,2,1,0:T(8,128)(2,1)}, u32[]{:S(2)}, u32[]{:S(2)}) collective-permute-start(bf16[3,1,2,2,384,384]{5,4,3,2,1,0:T(8,128)(2,1)} %pad_maximum_fusion.3), channel_id=1, source_target_pairs={{8,0},{16,8},{24,16},{9,1},{17,9},{25,17},{10,2},{18,10},{26,18},{... | collective-permute-start | bytes 10616840 | tf_op jit(solution)/shard_map/ppermute | solution.py:25
  174.8 5.0 copy-start.21
  182.0 4.1 copy-start.3
  182.8 2.1 copy-start
  186.0 6.2 slice-start
  188.3 3.9 slice-start.1
  204.7 4.5 copy-start.16
  211.1 0.7 copy-start.17
  214.0 4.1 copy-start.3
  214.8 2.1 copy-start
  218.1 6.2 slice-start
  220.3 3.9 slice-start.1
  236.7 4.5 copy-start.16
  243.1 0.7 copy-start.17
  254.4 4.0 copy-start.4
  255.3 2.1 copy-start.1
  258.5 6.1 slice-start.2
  260.7 3.9 slice-start.3
  285.8 4.1 copy-start.4
  286.6 2.1 copy-start.1
  289.8 6.1 slice-start.2
  292.1 3.9 slice-start.3
  314.8 3.7 copy-start.19
  318.6 4.4 copy-start.11
  318.6 4.4 copy-start.15
  325.4 4.0 copy-start.5
  326.2 2.1 copy-start.2
  329.5 6.1 slice-start.4
  331.7 3.9 slice-start.5
  356.7 4.0 copy-start.5
  357.5 2.1 copy-start.2
  360.8 6.1 slice-start.4
  363.0 3.9 slice-start.5
  385.8 3.1 copy-start.7
  388.3 2.1 copy-start.8
  389.2 2.3 copy-start.6
  390.8 1.7 copy-start.9
  390.8 2.2 copy-start.10
  395.4 114.7 %collective-permute-start.4 = (bf16[3,2,2,384,384]{4,3,2,1,0:T(8,128)(2,1)S(1)}, bf16[3,2,2,384,384]{4,3,2,1,0:T(8,128)(2,1)S(1)}, u32[]{:S(2)}, u32[]{:S(2)}) collective-permute-start(bf16[3,2,2,384,384]{4,3,2,1,0:T(8,128)(2,1)S(1)} %get-tuple-element.227), channel_id=1, source_target_pairs={{0,8},{8,16},{16,24},{1,9},{9,17},{17,25},{2,10},{10,18},{18,26},{... | collective-permute-start | bytes 10616840 | tf_op jit(solution)/shard_map/ppermute | solution.py:14
  471.3 120.5 %collective-permute-start.5 = (bf16[3,2,2,384,384]{4,3,2,1,0:T(8,128)(2,1)S(1)}, bf16[3,2,2,384,384]{4,3,2,1,0:T(8,128)(2,1)S(1)}, u32[]{:S(2)}, u32[]{:S(2)}) collective-permute-start(bf16[3,2,2,384,384]{4,3,2,1,0:T(8,128)(2,1)S(1)} %get-tuple-element.228), channel_id=1, source_target_pairs={{8,0},{16,8},{24,16},{9,1},{17,9},{25,17},{10,2},{18,10},{26,18},{... | collective-permute-start | bytes 10616840 | tf_op jit(solution)/shard_map/ppermute | solution.py:14
  592.6 110.6 %collective-permute-start.6 = (bf16[3,2,2,384,384]{4,3,2,1,0:T(8,128)(2,1)S(1)}, bf16[3,2,2,384,384]{4,3,2,1,0:T(8,128)(2,1)S(1)}, u32[]{:S(2)}, u32[]{:S(2)}) collective-permute-start(bf16[3,2,2,384,384]{4,3,2,1,0:T(8,128)(2,1)S(1)} %pad_maximum_fusion.4), channel_id=1, source_target_pairs={{32,0},{64,32},{96,64},{128,96},{160,128},{192,160},{224,192},{33,... | collective-permute-start | bytes 10616840 | tf_op jit(solution)/shard_map/ppermute | solution.py:14
  626.3 2.5 copy-start.18
  626.3 2.5 copy-start.20
  626.8 158.3 %collective-permute-start.7 = (bf16[3,2,2,384,384]{4,3,2,1,0:T(8,128)(2,1)S(1)}, bf16[3,2,2,384,384]{4,3,2,1,0:T(8,128)(2,1)S(1)}, u32[]{:S(2)}, u32[]{:S(2)}) collective-permute-start(bf16[3,2,2,384,384]{4,3,2,1,0:T(8,128)(2,1)S(1)} %pad_maximum_fusion.5), channel_id=1, source_target_pairs={{0,32},{32,64},{64,96},{96,128},{128,160},{160,192},{192,224},{1,3... | collective-permute-start | bytes 10616840 | tf_op jit(solution)/shard_map/ppermute | solution.py:14
where the time goes:
time: 799 us; the launch traced here: 788 us
  waiting for transfers between devices  399 us (50%)
  starting transfers between devices  128 us (16%)
  other arithmetic  99.3 us (12%)
  local copies, waits for them, and re-layouts  79.5 us (10%)
  matrix products  79.4 us (10%)
    ppermute x4, waiting for transfers between devices, from_behind(): lax.ppermute(value, axis, [(source, source + steps) for source in range(i...  273 us
    ppermute x4, starting transfers between devices, from_behind(): lax.ppermute(value, axis, [(source, source + steps) for source in range(i...  113 us
    ppermute x2, waiting for transfers between devices, padded_2(): lax.ppermute(lax.slice_in_dim(block, block.shape[dim] - width, None, axis...  94.9 us
    ppermute x2, waiting for transfers between devices, padded_2(): lax.ppermute(lax.slice_in_dim(block, 0, width, axis=dim), axis, backward)  30.7 us
    dot_general x6, matrix products, tile_backward(): jnp.einsum('qnk,qd->nkd', low_probs, grad_tile, preferred_element_type=jn...  27.8 us
    scatter-add x6, other arithmetic, tile_backward(): key_sum = running[0].at[picked].add(jnp.where(live_mask, key_terms, 0.0))  26.9 us
    scatter-add x6, other arithmetic, tile_backward(): running[1].at[picked].add(jnp.where(live_mask, value_terms, 0.0))  26.9 us
    dot_general x6, matrix products, tile_backward(): jnp.einsum('qd,nkd->qnk', grad_tile, values_used, preferred_element_type=...  23.3 us
  transfers between devices with their start and end apart: 8, of which 8 were waited for; matrix products, arithmetic and copies ran while one was open for 1% of the time, Pallas kernels for 0%

commit v1 on v0

v1 whole, which is shorter than its diff:
```python
import functools

import jax
import jax.numpy as jnp
from jax import lax
from jax.experimental import pallas as pl
from jax.experimental.pallas import tpu as pltpu
from jax.sharding import PartitionSpec as P

HD = 128
SLOTS = 9
UNUSED = 1e30
SAME_M, OWN, SAME_P, OTHER_M, OTHER_0, OTHER_P, CROSS_M, CROSS_0, CROSS_P = range(9)
FIRST_ORDER = (OWN, OTHER_0, OTHER_M, SAME_M, SAME_P, OTHER_P, CROSS_0, CROSS_M, CROSS_P)
SECOND_ORDER = (CROSS_P, CROSS_M, CROSS_0, SAME_P, OTHER_P, SAME_M, OTHER_M, OTHER_0, OWN)
SEND_OWN, RELAY_1, RELAY_2, RELAY_3 = 0, 3, 6, 9
FIRST = 13
MERGE = FIRST + 10
SECOND = FIRST + 13
RET_OTHER_P = SECOND + 5
RET_OTHER_M = SECOND + 7
RET_SAME_M = SECOND + 8
RET_OTHER_0 = SECOND + 11
RET_OWN = SECOND + 14
MESH = pl.DeviceIdType.MESH


def mirror(slot):
    return 2 - slot if slot < 3 else slot


def pick(table, index):
    value = jnp.int32(table[0])
    for k in range(1, len(table)):
        value = jnp.where(index == k, jnp.int32(table[k]), value)
    return value


def dot(a, b, dims):
    return lax.dot_general(a, b, (dims, ((), ())), preferred_element_type=jnp.float32)


def kernel(times, rows, heads, tile, q_hbm, k_hbm, v_hbm, g_hbm, mask, dq_hbm, dk_hbm, dv_hbm,
           fwd, keys, vals, keys_t, acc_k, acc_v, part, ret_out, ret_in, st_out, st_in, bc_out, bc_in,
           out_q, out_k, out_v, load_sem, fwd_s, fwd_r, st_s, st_r, bc_s, bc_r, ret_s, ret_r):
    chunk = fwd.shape[3]
    per_head = 2 * tile // chunk
    chunks = heads * per_head
    scale = HD ** -0.5
    scale2 = scale * 1.4426950408889634

    t, r = lax.axis_index("tm"), lax.axis_index("row")
    s = 1 - 2 * (t % 2)
    has_m = jnp.logical_and(r - s >= 0, r - s < rows)
    has_p = jnp.logical_and(r + s >= 0, r + s < rows)
    has_xo = jnp.logical_and(t + 2 * s >= 0, t + 2 * s < times)
    has_xi = jnp.logical_and(t - 2 * s >= 0, t - 2 * s < times)
    pair = {"tm": t + s, "row": r}
    outer = {"tm": t + s, "row": r - s}
    x_out = {"tm": t + 2 * s, "row": r}
    x_in = {"tm": t - 2 * s, "row": r}

    def both(a, b):
        return jnp.logical_and(a, b)

    row_ok = (has_m, True, has_p)

    def exists(slot):
        ok = row_ok[slot % 3]
        if slot // 3 == 2:
            ok = has_xi if ok is True else both(ok, has_xi)
        return ok

    def sent_to(slot):
        kind = (0, 1, -1)[slot // 3]
        return {"tm": t + s * kind, "row": r + s * (slot % 3 - 1)}

    def when(cond, fn):
        if cond is True:
            fn()
        else:
            pl.when(cond)(fn)

    loads = []
    for c in range(chunks):
        h, k = c // per_head, c % per_head
        for n, ref in enumerate((q_hbm, g_hbm)):
            loads.append(pltpu.make_async_copy(
                ref.at[pl.ds(k * chunk, chunk), pl.ds(h * HD, HD)], fwd.at[c, OWN, n], load_sem.at[len(loads)]))
    for h in range(heads):
        for ref, dst in ((k_hbm, keys), (v_hbm, vals)):
            loads.append(pltpu.make_async_copy(ref.at[:, pl.ds(h * HD, HD)], dst.at[h], load_sem.at[len(loads)]))
    for copy in loads:
        copy.start()

    barrier = pltpu.get_barrier_semaphore()
    greeted = [(sent_to(b), exists(b)) for b in range(SLOTS) if b != OWN] + [(x_out, has_xo), (x_in, has_xi)]
    count = jnp.int32(0)
    for device, ok in greeted:
        def greet(device=device):
            pl.semaphore_signal(barrier, inc=1, device_id=device, device_id_type=MESH)
        when(ok, greet)
        count = count + (1 if ok is True else ok.astype(jnp.int32))
    for copy in loads:
        copy.wait()
    for h in range(heads):
        keys_t[h] = keys[h].T
    acc_k[...] = jnp.zeros_like(acc_k)
    acc_v[...] = jnp.zeros_like(acc_v)
    pl.semaphore_wait(barrier, count)

    def fwd_copy(c, src, dst, device):
        return pltpu.make_async_remote_copy(
            src_ref=fwd.at[c, src], dst_ref=fwd.at[c, dst], send_sem=fwd_s.at[c, dst], recv_sem=fwd_r.at[c, dst],
            device_id=device, device_id_type=MESH)

    def st_copy(c, slot):
        return pltpu.make_async_remote_copy(
            src_ref=st_out.at[c, slot], dst_ref=st_in.at[c, mirror(slot)], send_sem=st_s.at[c, slot],
            recv_sem=st_r.at[c, mirror(slot)], device_id=sent_to(slot), device_id_type=MESH)

    def bc_copy(c, slot):
        return pltpu.make_async_remote_copy(
            src_ref=bc_out.at[c, slot], dst_ref=bc_in.at[c, mirror(slot)], send_sem=bc_s.at[c, slot],
            recv_sem=bc_r.at[c, mirror(slot)], device_id=sent_to(slot), device_id_type=MESH)

    def ret_copy(c, slot, device):
        return pltpu.make_async_remote_copy(
            src_ref=ret_out.at[c, slot], dst_ref=ret_in.at[c, slot], send_sem=ret_s.at[c, slot],
            recv_sem=ret_r.at[c, slot], device_id=device, device_id_type=MESH)

    def local_wait(buf, sems, c, slot):
        pltpu.make_async_copy(buf.at[c, slot], buf.at[c, slot], sems.at[c, slot]).wait()

    fwd_plan = (
        (OWN, OTHER_0, pair, True), (OWN, OTHER_M, outer, has_m),
        (OTHER_0, SAME_M, outer, has_m), (OTHER_0, CROSS_0, x_out, has_xo),
        (OTHER_M, SAME_P, pair, has_m), (OTHER_M, CROSS_M, x_out, both(has_m, has_xo)),
        (SAME_M, OTHER_P, pair, has_m), (OTHER_P, CROSS_P, x_out, both(has_p, has_xo)),
    )
    ret_device = {
        CROSS_P: x_in, CROSS_M: x_in, CROSS_0: x_in, SAME_P: pair, OTHER_P: pair,
        SAME_M: outer, OTHER_M: outer, OTHER_0: pair,
    }
    ret_adds = {
        OTHER_P: ((CROSS_P, has_xo),), SAME_M: ((OTHER_P, True),), OTHER_M: ((CROSS_M, has_xo), (SAME_P, True)),
        OTHER_0: ((CROSS_0, has_xo), (SAME_M, has_m)), OWN: ((OTHER_M, has_m), (OTHER_0, True)),
    }

    def send_fwd(c, src):
        for a, b, device, ok in fwd_plan:
            if a == src:
                when(ok, lambda a=a, b=b, device=device: fwd_copy(c, a, b, device).start())

    def relay(c, src):
        def go():
            local_wait(fwd, fwd_r, c, src)
            send_fwd(c, src)
        when(exists(src), go)

    def first_pass(c, slot):
        h = c // per_head
        q = fwd[c, slot, 0]
        g = fwd[c, slot, 1]
        for j in range(2):
            sc = dot(keys[h, pl.ds(j * tile, tile), :], q, ((1,), (1,)))
            peak = jnp.max(sc, axis=0, keepdims=True) * scale2
            e = jnp.exp2(sc * scale2 - peak)
            dp = dot(vals[h, pl.ds(j * tile, tile), :], g, ((1,), (1,)))
            st_out[c, slot, pl.ds(j, 1), :] = peak
            st_out[c, slot, pl.ds(2 + j, 1), :] = jnp.sum(e, axis=0, keepdims=True)
            st_out[c, slot, pl.ds(4 + j, 1), :] = jnp.sum(e * dp, axis=0, keepdims=True)

    def merge(c):
        for slot in range(SLOTS):
            if slot != OWN:
                when(exists(slot), lambda slot=slot: local_wait(st_in, st_r, c, slot))
        k = c % per_head

        def entry(slot, row):
            ref = st_out if slot == OWN else st_in
            return ref[c, slot, pl.ds(row, 2), :]

        used = [mask[k, slot, pl.ds(0, 2), :] > 0.5 for slot in range(SLOTS)]
        peaks = [jnp.where(used[slot], entry(slot, 0), -UNUSED) for slot in range(SLOTS)]
        top = functools.reduce(jnp.maximum, peaks)
        top = jnp.max(top, axis=0, keepdims=True)
        total = jnp.zeros_like(peaks[0])
        delta = jnp.zeros_like(peaks[0])
        for slot in range(SLOTS):
            w = jnp.exp2(peaks[slot] - top)
            total = total + jnp.where(used[slot], w * entry(slot, 2), 0.0)
            delta = delta + jnp.where(used[slot], w * entry(slot, 4), 0.0)
        total = jnp.sum(total, axis=0, keepdims=True)
        delta = jnp.sum(delta, axis=0, keepdims=True) / total
        lse = top + jnp.log2(total)
        for slot in range(SLOTS):
            ref = bc_in if slot == OWN else bc_out
            ref[c, slot, pl.ds(0, 2), :] = jnp.where(used[slot], lse, UNUSED)
            ref[c, slot, pl.ds(2, 1), :] = delta
        for slot in range(SLOTS):
            if slot != OWN:
                when(exists(slot), lambda slot=slot: bc_copy(c, slot).start())

    def second_pass(c, slot):
        h = c // per_head
        q = fwd[c, slot, 0]
        g = fwd[c, slot, 1]
        delta = bc_in[c, slot, pl.ds(2, 1), :]
        dq_t = None
        for j in range(2):
            span = pl.ds(j * tile, tile)
            sc = dot(keys[h, span, :], q, ((1,), (1,)))
            p = jnp.exp2(sc * scale2 - bc_in[c, slot, pl.ds(j, 1), :])
            dp = dot(vals[h, span, :], g, ((1,), (1,)))
            ds = (p * (dp - delta)).astype(jnp.bfloat16)
            acc_v[h, span, :] += dot(p.astype(jnp.bfloat16), g, ((1,), (0,)))
            acc_k[h, span, :] += dot(ds, q, ((1,), (0,)))
            term = dot(keys_t[h, :, span], ds, ((1,), (0,)))
            dq_t = term if dq_t is None else dq_t + term
        part[c % 2, slot] = dq_t

    def hand_back(c, slot):
        def go():
            for src, ok in ret_adds.get(slot, ()):
                def add(src=src):
                    local_wait(ret_in, ret_r, c, src)
                    part[c % 2, slot] += ret_in[c, src].astype(jnp.float32)
                when(ok, add)
            if slot == OWN:
                rows_at = pl.multiple_of((c % per_head) * chunk, chunk)
                out_q[c // per_head, pl.ds(rows_at, chunk), :] = (part[c % 2, slot] * scale).T.astype(jnp.bfloat16)
            else:
                ret_out[c, slot] = part[c % 2, slot].astype(jnp.bfloat16)
                ret_copy(c, slot, ret_device[slot]).start()
        when(exists(slot), go)

    def at(u, offset, fn):
        c = (u - offset) // SLOTS
        pl.when(both(u >= offset, both((u - offset) % SLOTS == 0, c < chunks)))(lambda: fn(c))

    def exists_dyn(slot):
        a = slot % 3
        ok = jnp.logical_or(a != 0, has_m)
        ok = both(ok, jnp.logical_or(a != 2, has_p))
        return both(ok, jnp.logical_or(slot // 3 != 2, has_xi))

    def step(u, carry):
        at(u, SEND_OWN, lambda c: send_fwd(c, OWN))

        def relay_1(c):
            relay(c, OTHER_0)
            relay(c, OTHER_M)

        at(u, RELAY_1, relay_1)
        at(u, RELAY_2, lambda c: relay(c, SAME_M))
        at(u, RELAY_3, lambda c: relay(c, OTHER_P))

        for slot in (SAME_P, CROSS_0, CROSS_M, CROSS_P):
            at(u, FIRST + FIRST_ORDER.index(slot),
               lambda c, slot=slot: when(exists(slot), lambda: local_wait(fwd, fwd_r, c, slot)))
        c1 = (u - FIRST) // SLOTS
        b1 = pick(FIRST_ORDER, (u - FIRST) % SLOTS)

        @pl.when(both(both(u >= FIRST, c1 < chunks), exists_dyn(b1)))
        def _():
            first_pass(c1, b1)

        for slot in FIRST_ORDER[1:]:
            at(u, FIRST + FIRST_ORDER.index(slot),
               lambda c, slot=slot: when(exists(slot), lambda: st_copy(c, slot).start()))

        at(u, MERGE, merge)

        for slot in SECOND_ORDER[:-1]:
            at(u, SECOND + SECOND_ORDER.index(slot),
               lambda c, slot=slot: when(exists(slot), lambda: local_wait(bc_in, bc_r, c, slot)))
        c2 = (u - SECOND) // SLOTS
        b2 = pick(SECOND_ORDER, (u - SECOND) % SLOTS)

        @pl.when(both(both(u >= SECOND, c2 < chunks), exists_dyn(b2)))
        def _():
            second_pass(c2, b2)

        for slot in SECOND_ORDER[:4]:
            at(u, SECOND + SECOND_ORDER.index(slot), lambda c, slot=slot: hand_back(c, slot))
        at(u, RET_OTHER_P, lambda c: hand_back(c, OTHER_P))
        at(u, RET_OTHER_M, lambda c: hand_back(c, OTHER_M))
        at(u, RET_SAME_M, lambda c: hand_back(c, SAME_M))
        at(u, RET_OTHER_0, lambda c: hand_back(c, OTHER_0))
        at(u, RET_OWN, lambda c: hand_back(c, OWN))
        return carry

    lax.fori_loop(0, RET_OWN + SLOTS * (chunks - 1) + 1, step, 0)

    out_k[...] = (acc_k[...] * scale).astype(jnp.bfloat16)
    out_v[...] = acc_v[...].astype(jnp.bfloat16)
    stores = []
    for h in range(heads):
        for src, ref in ((out_q, dq_hbm), (out_k, dk_hbm), (out_v, dv_hbm)):
            stores.append(pltpu.make_async_copy(src.at[h], ref.at[:, pl.ds(h * HD, HD)], load_sem.at[len(stores)]))
    for copy in stores:
        copy.start()

    def drain(c, carry):
        for a, b, device, ok in fwd_plan:
            when(ok, lambda a=a, b=b, device=device: fwd_copy(c, a, b, device).wait_send())
        for slot in range(SLOTS):
            if slot != OWN:
                def go(slot=slot):
                    st_copy(c, slot).wait_send()
                    bc_copy(c, slot).wait_send()
                    ret_copy(c, slot, ret_device[slot]).wait_send()
                when(exists(slot), go)
        return carry

    lax.fori_loop(0, chunks, drain, 0)
    for copy in stores:
        copy.wait()


def per_device(times, rows, query, key_tiles, value_tiles, grad_out, neighbours):
    _, _, count, tile, channels = query.shape
    heads = channels // HD
    tokens = count * tile
    per_head = 3
    chunk = tokens // per_head
    chunks = heads * per_head
    entries = neighbours[0, 0]
    listed = jnp.any(entries[:, :, None] == jnp.arange(9 * count, dtype=jnp.int32), axis=1)
    listed = listed.reshape(count, 9, count).astype(jnp.float32)
    place = [3 * (0, 1, -1)[slot // 3] + slot % 3 - 1 for slot in range(SLOTS)]
    even = jnp.stack([listed[:, 4 + p] for p in place])
    odd = jnp.stack([listed[:, 4 - p] for p in place])
    listed = jnp.where(lax.axis_index("tm") % 2 == 0, even, odd)
    mask = jnp.repeat(jnp.swapaxes(listed, 1, 2), tile, axis=2)
    mask = mask.reshape(SLOTS, count, per_head, chunk).transpose(2, 0, 1, 3)
    mask = jnp.pad(mask, ((0, 0), (0, 0), (0, 6), (0, 0)))

    flat = [value.reshape(tokens, channels) for value in (query, key_tiles, value_tiles, grad_out)]
    out = jax.ShapeDtypeStruct((tokens, channels), jnp.bfloat16)
    dma = pltpu.SemaphoreType.DMA
    vmem = pltpu.VMEM
    small = (chunks, SLOTS, 8, chunk)
    grads = pl.pallas_call(
        functools.partial(kernel, times, rows, heads, tile),
        out_shape=(out, out, out),
        in_specs=[pl.BlockSpec(memory_space=pl.ANY)] * 4 + [pl.BlockSpec(memory_space=pltpu.VMEM)],
        out_specs=[pl.BlockSpec(memory_space=pl.ANY)] * 3,
        scratch_shapes=[
            vmem((chunks, SLOTS, 2, chunk, HD), jnp.bfloat16),
            vmem((heads, tokens, HD), jnp.bfloat16),
            vmem((heads, tokens, HD), jnp.bfloat16),
            vmem((heads, HD, tokens), jnp.bfloat16),
            vmem((heads, tokens, HD), jnp.float32),
            vmem((heads, tokens, HD), jnp.float32),
            vmem((2, SLOTS, HD, chunk), jnp.float32),
            vmem((chunks, SLOTS, HD, chunk), jnp.bfloat16),
            vmem((chunks, SLOTS, HD, chunk), jnp.bfloat16),
            vmem(small, jnp.float32),
            vmem(small, jnp.float32),
            vmem(small, jnp.float32),
            vmem(small, jnp.float32),
            vmem((heads, tokens, HD), jnp.bfloat16),
            vmem((heads, tokens, HD), jnp.bfloat16),
            vmem((heads, tokens, HD), jnp.bfloat16),
            dma((2 * chunks + 2 * heads,)),
        ] + [dma((chunks, SLOTS))] * 8,
        compiler_params=pltpu.CompilerParams(
            collective_id=0, has_side_effects=True, vmem_limit_bytes=56 * 1024 * 1024
        ),
    )(flat[0], flat[1], flat[2], flat[3], mask)
    return tuple(grad.reshape(query.shape) for grad in grads)


def solution(mesh):
    spec = P("tm", "row", None, None, "head")
    return jax.shard_map(
        functools.partial(per_device, mesh.shape["tm"], mesh.shape["row"]),
        mesh=mesh,
        in_specs=(spec, spec, spec, spec, P("tm", "row", None, None)),
        out_specs=(spec, spec, spec),
        check_vma=False,
    )
```

time: 799 us -> 236 us (0.30); the launches traced: 788 us -> 235 us
  waiting for transfers between devices: 399 us -> 0 us
  Pallas kernels: 0 us -> 227 us
  starting transfers between devices: 128 us -> 0 us
  other arithmetic: 99.3 us -> 0.1 us
  matrix products: 79.4 us -> 0 us
  local copies, waits for them, and re-layouts: 79.5 us -> 6.94 us
    ppermute x8 -> x0, waiting for transfers between devices: 399 us -> none  [the longest x4 273 us: from_behind(): lax.ppermute(value, axis, [(source, source + steps) for source in range(i...]
    pallas_call x0 -> x1, Pallas kernels: none -> 227 us  [per_device(): pl.pallas_call(functools.partial(kernel, times, rows, heads, tile), out_s...]
    ppermute x8 -> x0, starting transfers between devices: 128 us -> none  [the longest x4 113 us: from_behind(): lax.ppermute(value, axis, [(source, source + steps) for source in range(i...]
    dot_general x30 -> x0, matrix products: 79.4 us -> none  [the longest x6 27.8 us: tile_backward(): jnp.einsum('qnk,qd->nkd', low_probs, grad_tile, preferred_element_type=jn...]
    scatter-add x12 -> x0, other arithmetic: 53.9 us -> none  [the longest x6 26.9 us: tile_backward(): key_sum = running[0].at[picked].add(jnp.where(live_mask, key_terms, 0.0))]
    gather x12 -> x0, local copies, waits for them, and re-layouts: 26.4 us -> none  [the longest x6 13.4 us: tile_backward(): values_used = value_head[picked]]
    slice x5 -> x1, local copies, waits for them, and re-layouts: 20.3 us -> 0.01 us  [per_device(): even = jnp.stack([listed[:, 4 + p] for p in place])]
    concatenate x5 -> x0, other arithmetic: 14.6 us -> none  [the longest x2 12.3 us: padded_2(): block = jnp.concatenate([low, block, high], axis=dim)]
  transfers between devices with their start and end apart: 8 -> 0, of which waited for: 8 -> 0; matrix products, arithmetic and copies ran while one was open for 1% -> 0% of each run, Pallas kernels for 0% -> 0%
where the time goes in v1:
time: 236 us; the launch traced here: 235 us
  Pallas kernels  227 us (96%)
  local copies, waits for them, and re-layouts  6.94 us (3%)
    pallas_call x1, Pallas kernels, per_device(): pl.pallas_call(functools.partial(kernel, times, rows, heads, tile), out_s...  227 us
    unnamed x9, local copies, waits for them, and re-layouts  4.77 us

profile of v1, /device:TPU:20, one launch (start us, length us, event | category | flops | bytes accessed | tf_op | source)
XLA Modules:
  0.0 234.7 jit_solution(2047543799923607452)
XLA Ops:
  0.6 0.0 copy-start.2
  0.7 0.7 copy-done.2
  1.3 0.1 fusion
  1.4 0.1 reshape.38
  1.5 0.1 copy.38
  1.6 0.1 copy.39
  1.7 0.1 copy.37
  1.8 0.1 copy.36
  1.9 0.1 copy.35
  2.0 0.1 copy.34
  2.1 0.1 copy.33
  2.2 0.1 copy.32
  2.3 0.1 copy.31
  2.4 0.1 stack.7
  2.5 0.1 stack.6
  2.6 0.1 copy.49
  2.7 0.1 broadcast_in_dim.4
  2.8 0.1 reshape_reshape.3
  2.9 0.7 pad.4.mask
  3.6 226.9 %shard_map.76 = (bf16[768,384]{1,0:T(8,128)(2,1)}, bf16[768,384]{1,0:T(8,128)(2,1)}, bf16[768,384]{1,0:T(8,128)(2,1)}) custom-call(bf16[768,384]{1,0:T(8,128)(2,1)} %bitcast.22, bf16[768,384]{1,0:T(8,128)(2,1)} %bitcast.23, bf16[768,384]{1,0:T(8,128)(2,1)} %bitcast.24, bf16[768,384]{1,0:T(8,128)(2,1)} %bitcast.25, f32[3,9,8,256]{3,2,1,0:T(8,128)} %pad.4.mask), custom_call_target="tpu_custom_call" | custom-call | tf_op jit(solution)/shard_map/pallas_call | solution.py:345
  230.6 0.0 copy-start.1
  230.6 2.0 copy.56
  232.6 0.0 copy-done.1
  232.6 0.0 copy-start
  232.6 0.8 copy.57
  233.4 0.5 copy-done
  233.9 0.8 copy.58
  (4 shorter events, 0.1 us)
Async XLA Ops:
  0.6 0.7 copy-start.2
  230.6 2.0 copy-start.1
  232.6 1.3 copy-start

commit v2 on v1

--- a/solution.py
+++ b/solution.py
@@ -13,20 +13,23 @@
 SAME_M, OWN, SAME_P, OTHER_M, OTHER_0, OTHER_P, CROSS_M, CROSS_0, CROSS_P = range(9)
 FIRST_ORDER = (OWN, OTHER_0, OTHER_M, SAME_M, SAME_P, OTHER_P, CROSS_0, CROSS_M, CROSS_P)
 SECOND_ORDER = (CROSS_P, CROSS_M, CROSS_0, SAME_P, OTHER_P, SAME_M, OTHER_M, OTHER_0, OWN)
-SEND_OWN, RELAY_1, RELAY_2, RELAY_3 = 0, 3, 6, 9
-FIRST = 13
-MERGE = FIRST + 10
-SECOND = FIRST + 13
-RET_OTHER_P = SECOND + 5
-RET_OTHER_M = SECOND + 7
-RET_SAME_M = SECOND + 8
-RET_OTHER_0 = SECOND + 11
-RET_OWN = SECOND + 14
+SEND_OWN, RELAY_1, RELAY_2, RELAY_3 = 0, 6, 12, 18
+FIRST = 22
+MERGE = FIRST + 14
+SECOND = FIRST + 20
+RET_OTHER_P = SECOND + 7
+RET_OTHER_M = SECOND + 10
+RET_SAME_M = SECOND + 12
+RET_OTHER_0 = SECOND + 18
+RET_OWN = SECOND + 24
+TAKE_MARKS = 2
 MESH = pl.DeviceIdType.MESH
 
 
 def mirror(slot):
-    return 2 - slot if slot < 3 else slot
+    if isinstance(slot, int):
+        return 2 - slot if slot < 3 else slot
+    return jnp.where(slot < 3, 2 - slot, slot)
 
 
 def pick(table, index):
@@ -40,9 +43,9 @@
     return lax.dot_general(a, b, (dims, ((), ())), preferred_element_type=jnp.float32)
 
 
-def kernel(times, rows, heads, tile, q_hbm, k_hbm, v_hbm, g_hbm, mask, dq_hbm, dk_hbm, dv_hbm,
+def kernel(times, rows, heads, tile, q_hbm, k_hbm, v_hbm, g_hbm, mark_out, dq_hbm, dk_hbm, dv_hbm,
            fwd, keys, vals, keys_t, acc_k, acc_v, part, ret_out, ret_in, st_out, st_in, bc_out, bc_in,
-           out_q, out_k, out_v, load_sem, fwd_s, fwd_r, st_s, st_r, bc_s, bc_r, ret_s, ret_r):
+           out_q, out_k, out_v, load_sem, fwd_s, fwd_r, st_s, st_r, bc_s, bc_r, ret_s, ret_r, low_p, low_ds, mark_in, marks, mark_s, mark_r):
     chunk = fwd.shape[3]
     per_head = 2 * tile // chunk
     chunks = heads * per_head
@@ -72,7 +75,7 @@
         return ok
 
     def sent_to(slot):
-        kind = (0, 1, -1)[slot // 3]
+        kind = (slot // 3 + 1) % 3 - 1
         return {"tm": t + s * kind, "row": r + s * (slot % 3 - 1)}
 
     def when(cond, fn):
@@ -121,7 +124,7 @@
 
     def bc_copy(c, slot):
         return pltpu.make_async_remote_copy(
-            src_ref=bc_out.at[c, slot], dst_ref=bc_in.at[c, mirror(slot)], send_sem=bc_s.at[c, slot],
+            src_ref=bc_out.at[c, 0], dst_ref=bc_in.at[c, mirror(slot)], send_sem=bc_s.at[c, slot],
             recv_sem=bc_r.at[c, mirror(slot)], device_id=sent_to(slot), device_id_type=MESH)
 
     def ret_copy(c, slot, device):
@@ -131,6 +134,24 @@
 
     def local_wait(buf, sems, c, slot):
         pltpu.make_async_copy(buf.at[c, slot], buf.at[c, slot], sems.at[c, slot]).wait()
+
+    def mark_copy(slot):
+        return pltpu.make_async_remote_copy(
+            src_ref=mark_out.at[slot], dst_ref=mark_in.at[mirror(slot)], send_sem=mark_s.at[slot],
+            recv_sem=mark_r.at[mirror(slot)], device_id=sent_to(slot), device_id_type=MESH)
+
+    def take_marks(c):
+        for slot in range(SLOTS):
+            if slot != OWN:
+                when(exists(slot), lambda slot=slot: pltpu.make_async_copy(
+                    mark_in.at[slot], mark_in.at[slot], mark_r.at[slot]).wait())
+        half = chunk // 2
+        for slot in range(SLOTS):
+            ref = mark_out if slot == OWN else mark_in
+            for k in range(per_head):
+                for n in range(2):
+                    i = (2 * k + n) // per_head
+                    marks[k, slot, :, pl.ds(n * half, half)] = ref[slot, pl.ds(2 * i, 2), :]
 
     fwd_plan = (
         (OWN, OTHER_0, pair, True), (OWN, OTHER_M, outer, has_m),
@@ -162,42 +183,45 @@
         h = c // per_head
         q = fwd[c, slot, 0]
         g = fwd[c, slot, 1]
+        parts = []
         for j in range(2):
-            sc = dot(keys[h, pl.ds(j * tile, tile), :], q, ((1,), (1,)))
-            peak = jnp.max(sc, axis=0, keepdims=True) * scale2
-            e = jnp.exp2(sc * scale2 - peak)
-            dp = dot(vals[h, pl.ds(j * tile, tile), :], g, ((1,), (1,)))
-            st_out[c, slot, pl.ds(j, 1), :] = peak
-            st_out[c, slot, pl.ds(2 + j, 1), :] = jnp.sum(e, axis=0, keepdims=True)
-            st_out[c, slot, pl.ds(4 + j, 1), :] = jnp.sum(e * dp, axis=0, keepdims=True)
+            used = marks[c % per_head, slot, pl.ds(j, 1), :] > 0.5
+            for i in range(3):
+                span = pl.ds(j * tile + i * (tile // 3), tile // 3)
+                sc = dot(keys[h, span, :], q, ((1,), (1,)))
+                peak = jnp.max(sc, axis=0, keepdims=True) * scale2
+                e = jnp.exp2(sc * scale2 - peak)
+                dp = dot(vals[h, span, :], g, ((1,), (1,)))
+                parts.append((used, jnp.where(used, peak, -UNUSED), jnp.sum(e, axis=0, keepdims=True),
+                              jnp.sum(e * dp, axis=0, keepdims=True)))
+        top = functools.reduce(jnp.maximum, [peak for _, peak, _, _ in parts])
+        ws = [jnp.where(used, jnp.exp2(peak - top), 0.0) for used, peak, _, _ in parts]
+        total = sum(w * item[2] for w, item in zip(ws, parts))
+        mean = sum(w * item[3] for w, item in zip(ws, parts))
+        some = jnp.logical_or(parts[0][0], parts[3][0])
+        total = jnp.where(some, total, 1.0)
+        st_out[c, slot, pl.ds(0, 1), :] = jnp.where(some, top + jnp.log2(total), -UNUSED)
+        st_out[c, slot, pl.ds(1, 1), :] = jnp.where(some, mean / total, 0.0)
 
     def merge(c):
         for slot in range(SLOTS):
             if slot != OWN:
                 when(exists(slot), lambda slot=slot: local_wait(st_in, st_r, c, slot))
-        k = c % per_head
-
-        def entry(slot, row):
+        lses, means = [], []
+        for slot in range(SLOTS):
             ref = st_out if slot == OWN else st_in
-            return ref[c, slot, pl.ds(row, 2), :]
-
-        used = [mask[k, slot, pl.ds(0, 2), :] > 0.5 for slot in range(SLOTS)]
-        peaks = [jnp.where(used[slot], entry(slot, 0), -UNUSED) for slot in range(SLOTS)]
-        top = functools.reduce(jnp.maximum, peaks)
-        top = jnp.max(top, axis=0, keepdims=True)
-        total = jnp.zeros_like(peaks[0])
-        delta = jnp.zeros_like(peaks[0])
-        for slot in range(SLOTS):
-            w = jnp.exp2(peaks[slot] - top)
-            total = total + jnp.where(used[slot], w * entry(slot, 2), 0.0)
-            delta = delta + jnp.where(used[slot], w * entry(slot, 4), 0.0)
-        total = jnp.sum(total, axis=0, keepdims=True)
-        delta = jnp.sum(delta, axis=0, keepdims=True) / total
+            lse, mean = ref[c, slot, pl.ds(0, 1), :], ref[c, slot, pl.ds(1, 1), :]
+            ok = exists(slot)
+            lses.append(lse if ok is True else jnp.where(ok, lse, -UNUSED))
+            means.append(mean if ok is True else jnp.where(ok, mean, 0.0))
+        top = functools.reduce(jnp.maximum, lses)
+        ws = [jnp.exp2(lse - top) for lse in lses]
+        total = sum(ws)
         lse = top + jnp.log2(total)
-        for slot in range(SLOTS):
-            ref = bc_in if slot == OWN else bc_out
-            ref[c, slot, pl.ds(0, 2), :] = jnp.where(used[slot], lse, UNUSED)
-            ref[c, slot, pl.ds(2, 1), :] = delta
+        delta = sum(w * mean for w, mean in zip(ws, means)) / total
+        for ref, slot in ((bc_out, 0), (bc_in, OWN)):
+            ref[c, slot, pl.ds(0, 1), :] = lse
+            ref[c, slot, pl.ds(1, 1), :] = delta
         for slot in range(SLOTS):
             if slot != OWN:
                 when(exists(slot), lambda slot=slot: bc_copy(c, slot).start())
@@ -206,19 +230,19 @@
         h = c // per_head
         q = fwd[c, slot, 0]
         g = fwd[c, slot, 1]
-        delta = bc_in[c, slot, pl.ds(2, 1), :]
-        dq_t = None
+        lse = bc_in[c, slot, pl.ds(0, 1), :]
+        delta = bc_in[c, slot, pl.ds(1, 1), :]
+        sc = dot(keys[h], q, ((1,), (1,)))
+        dp = dot(vals[h], g, ((1,), (1,)))
         for j in range(2):
-            span = pl.ds(j * tile, tile)
-            sc = dot(keys[h, span, :], q, ((1,), (1,)))
-            p = jnp.exp2(sc * scale2 - bc_in[c, slot, pl.ds(j, 1), :])
-            dp = dot(vals[h, span, :], g, ((1,), (1,)))
-            ds = (p * (dp - delta)).astype(jnp.bfloat16)
-            acc_v[h, span, :] += dot(p.astype(jnp.bfloat16), g, ((1,), (0,)))
-            acc_k[h, span, :] += dot(ds, q, ((1,), (0,)))
-            term = dot(keys_t[h, :, span], ds, ((1,), (0,)))
-            dq_t = term if dq_t is None else dq_t + term
-        part[c % 2, slot] = dq_t
+            span = slice(j * tile, (j + 1) * tile)
+            used = marks[c % per_head, slot, pl.ds(j, 1), :] > 0.5
+            p = jnp.exp2(sc[span] * scale2 - jnp.where(used, lse, UNUSED))
+            low_p[pl.ds(j * tile, tile), :] = p.astype(jnp.bfloat16)
+            low_ds[pl.ds(j * tile, tile), :] = (p * (dp[span] - delta)).astype(jnp.bfloat16)
+        acc_v[h] += dot(low_p[...], g, ((1,), (0,)))
+        acc_k[h] += dot(low_ds[...], q, ((1,), (0,)))
+        return dot(keys_t[h], low_ds[...], ((1,), (0,)))
 
     def hand_back(c, slot):
         def go():
@@ -235,63 +259,92 @@
                 ret_copy(c, slot, ret_device[slot]).start()
         when(exists(slot), go)
 
-    def at(u, offset, fn):
-        c = (u - offset) // SLOTS
-        pl.when(both(u >= offset, both((u - offset) % SLOTS == 0, c < chunks)))(lambda: fn(c))
-
     def exists_dyn(slot):
         a = slot % 3
         ok = jnp.logical_or(a != 0, has_m)
         ok = both(ok, jnp.logical_or(a != 2, has_p))
         return both(ok, jnp.logical_or(slot // 3 != 2, has_xi))
 
-    def step(u, carry):
-        at(u, SEND_OWN, lambda c: send_fwd(c, OWN))
-
-        def relay_1(c):
-            relay(c, OTHER_0)
-            relay(c, OTHER_M)
-
-        at(u, RELAY_1, relay_1)
-        at(u, RELAY_2, lambda c: relay(c, SAME_M))
-        at(u, RELAY_3, lambda c: relay(c, OTHER_P))
-
-        for slot in (SAME_P, CROSS_0, CROSS_M, CROSS_P):
-            at(u, FIRST + FIRST_ORDER.index(slot),
-               lambda c, slot=slot: when(exists(slot), lambda: local_wait(fwd, fwd_r, c, slot)))
-        c1 = (u - FIRST) // SLOTS
-        b1 = pick(FIRST_ORDER, (u - FIRST) % SLOTS)
-
-        @pl.when(both(both(u >= FIRST, c1 < chunks), exists_dyn(b1)))
+    def relay_1(c):
+        relay(c, OTHER_0)
+        relay(c, OTHER_M)
+
+    events = (
+        (SEND_OWN, lambda c: send_fwd(c, OWN)), (RELAY_1, relay_1), (RELAY_2, lambda c: relay(c, SAME_M)),
+        (RELAY_3, lambda c: relay(c, OTHER_P)), (MERGE, merge),
+        (RET_OTHER_P, lambda c: hand_back(c, OTHER_P)), (RET_OTHER_M, lambda c: hand_back(c, OTHER_M)),
+        (RET_SAME_M, lambda c: hand_back(c, SAME_M)), (RET_OTHER_0, lambda c: hand_back(c, OTHER_0)),
+        (RET_OWN, lambda c: hand_back(c, OWN)),
+    )
+
+    def place(it, b, offset):
+        late = b < offset % SLOTS
+        c = it - offset // SLOTS - late.astype(jnp.int32)
+        index = b - offset % SLOTS + jnp.where(late, SLOTS, 0)
+        return c, index, both(c >= 0, c < chunks)
+
+    for slot in range(SLOTS):
+        if slot != OWN:
+            when(exists(slot), lambda slot=slot: mark_copy(slot).start())
+
+    def step(it, b):
+        for k in range(SLOTS):
+            here = [(offset // SLOTS, fn) for offset, fn in events if offset % SLOTS == k]
+
+            def run(here=here):
+                for lag, fn in here:
+                    c = it - lag
+                    pl.when(both(c >= 0, c < chunks))(lambda fn=fn, c=c: fn(c))
+
+            if here:
+                pl.when(b == k)(run)
+
+        @pl.when(both(it == TAKE_MARKS // SLOTS, b == TAKE_MARKS % SLOTS))
         def _():
+            take_marks(0)
+
+        c1, i1, ok1 = place(it, b, FIRST)
+        b1 = pick(FIRST_ORDER, i1)
+
+        @pl.when(both(ok1, exists_dyn(b1)))
+        def _():
+            @pl.when(jnp.logical_or(i1 == FIRST_ORDER.index(SAME_P), i1 >= FIRST_ORDER.index(CROSS_0)))
+            def _():
+                local_wait(fwd, fwd_r, c1, b1)
+
             first_pass(c1, b1)
 
-        for slot in FIRST_ORDER[1:]:
-            at(u, FIRST + FIRST_ORDER.index(slot),
-               lambda c, slot=slot: when(exists(slot), lambda: st_copy(c, slot).start()))
-
-        at(u, MERGE, merge)
-
-        for slot in SECOND_ORDER[:-1]:
-            at(u, SECOND + SECOND_ORDER.index(slot),
-               lambda c, slot=slot: when(exists(slot), lambda: local_wait(bc_in, bc_r, c, slot)))
-        c2 = (u - SECOND) // SLOTS
-        b2 = pick(SECOND_ORDER, (u - SECOND) % SLOTS)
-
-        @pl.when(both(both(u >= SECOND, c2 < chunks), exists_dyn(b2)))
+            @pl.when(b1 != OWN)
+            def _():
+                st_copy(c1, b1).start()
+
+        c2, i2, ok2 = place(it, b, SECOND)
+        b2 = pick(SECOND_ORDER, i2)
+
+        @pl.when(both(ok2, exists_dyn(b2)))
         def _():
-            second_pass(c2, b2)
-
-        for slot in SECOND_ORDER[:4]:
-            at(u, SECOND + SECOND_ORDER.index(slot), lambda c, slot=slot: hand_back(c, slot))
-        at(u, RET_OTHER_P, lambda c: hand_back(c, OTHER_P))
-        at(u, RET_OTHER_M, lambda c: hand_back(c, OTHER_M))
-        at(u, RET_SAME_M, lambda c: hand_back(c, SAME_M))
-        at(u, RET_OTHER_0, lambda c: hand_back(c, OTHER_0))
-        at(u, RET_OWN, lambda c: hand_back(c, OWN))
-        return carry
-
-    lax.fori_loop(0, RET_OWN + SLOTS * (chunks - 1) + 1, step, 0)
+            @pl.when(b2 != OWN)
+            def _():
+                local_wait(bc_in, bc_r, c2, b2)
+
+            term = second_pass(c2, b2)
+
+            @pl.when(i2 >= 4)
+            def _():
+                part[c2 % 2, b2] = term
+
+            @pl.when(i2 < 4)
+            def _():
+                ret_out[c2, b2] = term.astype(jnp.bfloat16)
+                ret_copy(c2, b2, {"tm": jnp.where(i2 == 3, t + s, t - 2 * s), "row": r}).start()
+
+    def chunk_steps(it, carry):
+        def one(b, carry):
+            step(it, b)
+            return carry
+        return lax.fori_loop(0, SLOTS, one, carry)
+
+    lax.fori_loop(0, chunks + RET_OWN // SLOTS, chunk_steps, 0)
 
     out_k[...] = (acc_k[...] * scale).astype(jnp.bfloat16)
     out_v[...] = acc_v[...].astype(jnp.bfloat16)
@@ -315,6 +368,9 @@
         return carry
 
     lax.fori_loop(0, chunks, drain, 0)
+    for slot in range(SLOTS):
+        if slot != OWN:
+            when(exists(slot), lambda slot=slot: mark_copy(slot).wait_send())
     for copy in stores:
         copy.wait()
 
@@ -327,21 +383,17 @@
     chunk = tokens // per_head
     chunks = heads * per_head
     entries = neighbours[0, 0]
-    listed = jnp.any(entries[:, :, None] == jnp.arange(9 * count, dtype=jnp.int32), axis=1)
-    listed = listed.reshape(count, 9, count).astype(jnp.float32)
-    place = [3 * (0, 1, -1)[slot // 3] + slot % 3 - 1 for slot in range(SLOTS)]
-    even = jnp.stack([listed[:, 4 + p] for p in place])
-    odd = jnp.stack([listed[:, 4 - p] for p in place])
-    listed = jnp.where(lax.axis_index("tm") % 2 == 0, even, odd)
-    mask = jnp.repeat(jnp.swapaxes(listed, 1, 2), tile, axis=2)
-    mask = mask.reshape(SLOTS, count, per_head, chunk).transpose(2, 0, 1, 3)
-    mask = jnp.pad(mask, ((0, 0), (0, 0), (0, 6), (0, 0)))
+    place = jnp.array([3 * ((slot // 3 + 1) % 3 - 1) + slot % 3 - 1 for slot in range(SLOTS)], jnp.int32)
+    code = 4 + place * (1 - 2 * (lax.axis_index("tm") % 2))
+    names = code[:, None] * count + jnp.arange(count * count, dtype=jnp.int32) % count
+    listed = jnp.any(names[:, :, None] == jnp.repeat(entries, count, axis=0)[None], axis=2)
+    marks = jnp.broadcast_to(listed.astype(jnp.float32)[:, :, None], (SLOTS, count * count, chunk // 2))
 
     flat = [value.reshape(tokens, channels) for value in (query, key_tiles, value_tiles, grad_out)]
     out = jax.ShapeDtypeStruct((tokens, channels), jnp.bfloat16)
     dma = pltpu.SemaphoreType.DMA
     vmem = pltpu.VMEM
-    small = (chunks, SLOTS, 8, chunk)
+    small = (chunks, SLOTS, 2, chunk)
     grads = pl.pallas_call(
         functools.partial(kernel, times, rows, heads, tile),
         out_shape=(out, out, out),
@@ -359,17 +411,22 @@
             vmem((chunks, SLOTS, HD, chunk), jnp.bfloat16),
             vmem(small, jnp.float32),
             vmem(small, jnp.float32),
-            vmem(small, jnp.float32),
+            vmem((chunks, 1, 2, chunk), jnp.float32),
             vmem(small, jnp.float32),
             vmem((heads, tokens, HD), jnp.bfloat16),
             vmem((heads, tokens, HD), jnp.bfloat16),
             vmem((heads, tokens, HD), jnp.bfloat16),
             dma((2 * chunks + 2 * heads,)),
-        ] + [dma((chunks, SLOTS))] * 8,
+        ] + [dma((chunks, SLOTS))] * 8 + [vmem((tokens, chunk), jnp.bfloat16)] * 2 + [
+            vmem((SLOTS, count * count, chunk // 2), jnp.float32),
+            vmem((per_head, SLOTS, 2, chunk), jnp.float32),
+            dma((SLOTS,)),
+            dma((SLOTS,)),
+        ],
         compiler_params=pltpu.CompilerParams(
             collective_id=0, has_side_effects=True, vmem_limit_bytes=56 * 1024 * 1024
         ),
-    )(flat[0], flat[1], flat[2], flat[3], mask)
+    )(flat[0], flat[1], flat[2], flat[3], marks)
     return tuple(grad.reshape(query.shape) for grad in grads)
 
 

time: 236 us -> 170 us (0.72)
  Pallas kernels: 227 us -> 163 us
    pallas_call x1, Pallas kernels: 227 us -> 163 us  [per_device(): pl.pallas_call(functools.partial(kernel, times, rows, heads, tile), out_s...]
    unnamed x9 -> x11, local copies, waits for them, and re-layouts: 4.77 us -> 5.35 us
where the time goes in v2:
time: 170 us
  Pallas kernels  163 us (96%)
  local copies, waits for them, and re-layouts  6.13 us (4%)
    pallas_call x1, Pallas kernels, per_device(): pl.pallas_call(functools.partial(kernel, times, rows, heads, tile), out_s...  163 us
    unnamed x11, local copies, waits for them, and re-layouts  5.35 us

profile of v2, /device:TPU:20, one launch (start us, length us, event | category | flops | bytes accessed | tf_op | source)
XLA Modules:
  0.0 169.5 jit_solution(16686202325384493012)
XLA Ops:
  0.6 0.0 copy-start.3
  0.7 0.6 copy-done.3
  1.3 0.0 copy-start.2
  1.3 0.1 broadcast_add_fusion
  1.4 0.6 copy-done.2
  2.0 0.1 compare_reduce_fusion
  2.1 0.1 copy.9
  2.2 0.7 broadcast_in_dim.5.mark_out
  2.9 162.5 %shard_map.85 = (bf16[768,384]{1,0:T(8,128)(2,1)}, bf16[768,384]{1,0:T(8,128)(2,1)}, bf16[768,384]{1,0:T(8,128)(2,1)}) custom-call(bf16[768,384]{1,0:T(8,128)(2,1)} %bitcast.12, bf16[768,384]{1,0:T(8,128)(2,1)} %bitcast.13, bf16[768,384]{1,0:T(8,128)(2,1)} %bitcast.14, bf16[768,384]{1,0:T(8,128)(2,1)} %bitcast.15, f32[9,4,128]{2,1,0:T(4,128)} %broadcast_in_dim.5.mark_out), custom_call_target="tpu_custom_call" | custom-call | tf_op jit(solution)/shard_map/pallas_call | solution.py:397
  165.4 0.0 copy-start.1
  165.4 2.0 %copy.13 = bf16[1,1,2,384,384]{4,3,2,1,0:T(8,128)(2,1)} copy(bf16[1,1,2,384,384]{4,3,2,1,0:T(8,128)(2,1)} %bitcast.11) | data formatting | bytes 1179648
  167.4 0.0 copy-done.1
  167.4 0.0 copy-start
  167.4 0.8 copy.14
  168.2 0.5 copy-done
  168.7 0.8 copy.15
  (4 shorter events, 0.0 us)
Async XLA Ops:
  0.6 0.7 copy-start.3
  1.3 0.7 copy-start.2
  165.4 2.0 %copy-start.1 = (bf16[768,384]{1,0:T(8,128)(2,1)S(1)}, bf16[768,384]{1,0:T(8,128)(2,1)}, u32[]{:S(2)}) copy-start(bf16[768,384]{1,0:T(8,128)(2,1)} %get-tuple-element.7) | copy-start | bytes 1769476
  167.4 1.3 copy-start

commit v3 on v2

--- a/solution.py
+++ b/solution.py
@@ -11,18 +11,20 @@
 SLOTS = 9
 UNUSED = 1e30
 SAME_M, OWN, SAME_P, OTHER_M, OTHER_0, OTHER_P, CROSS_M, CROSS_0, CROSS_P = range(9)
-FIRST_ORDER = (OWN, OTHER_0, OTHER_M, SAME_M, SAME_P, OTHER_P, CROSS_0, CROSS_M, CROSS_P)
-SECOND_ORDER = (CROSS_P, CROSS_M, CROSS_0, SAME_P, OTHER_P, SAME_M, OTHER_M, OTHER_0, OWN)
+FIRST_ORDER = (OTHER_0, OTHER_M, SAME_M, SAME_P, OTHER_P, CROSS_0, CROSS_M, CROSS_P, OWN)
+SECOND_ORDER = (OWN, CROSS_P, CROSS_M, CROSS_0, SAME_P, OTHER_P, SAME_M, OTHER_M, OTHER_0)
 SEND_OWN, RELAY_1, RELAY_2, RELAY_3 = 0, 6, 12, 18
-FIRST = 22
-MERGE = FIRST + 14
-SECOND = FIRST + 20
-RET_OTHER_P = SECOND + 7
-RET_OTHER_M = SECOND + 10
-RET_SAME_M = SECOND + 12
-RET_OTHER_0 = SECOND + 18
-RET_OWN = SECOND + 24
-TAKE_MARKS = 2
+FIRST = 15
+MERGE = FIRST + 16
+SECOND = FIRST + 22
+RET_OTHER_P = SECOND + 8
+RET_OTHER_M = SECOND + 11
+RET_SAME_M = SECOND + 13
+RET_OTHER_0 = SECOND + 19
+RET_OWN = SECOND + 25
+STORE_KV = SECOND + 9
+DRAIN = RET_OWN + 1
+SET_UP = 2
 MESH = pl.DeviceIdType.MESH
 
 
@@ -45,7 +47,7 @@
 
 def kernel(times, rows, heads, tile, q_hbm, k_hbm, v_hbm, g_hbm, mark_out, dq_hbm, dk_hbm, dv_hbm,
            fwd, keys, vals, keys_t, acc_k, acc_v, part, ret_out, ret_in, st_out, st_in, bc_out, bc_in,
-           out_q, out_k, out_v, load_sem, fwd_s, fwd_r, st_s, st_r, bc_s, bc_r, ret_s, ret_r, low_p, low_ds, mark_in, marks, mark_s, mark_r):
+           out_q, out_k, out_v, load_sem, fwd_s, fwd_r, st_s, st_r, bc_s, bc_r, ret_s, ret_r, low_p, low_ds, mark_in, marks, mark_s, mark_r, store_sem):
     chunk = fwd.shape[3]
     per_head = 2 * tile // chunk
     chunks = heads * per_head
@@ -104,12 +106,6 @@
             pl.semaphore_signal(barrier, inc=1, device_id=device, device_id_type=MESH)
         when(ok, greet)
         count = count + (1 if ok is True else ok.astype(jnp.int32))
-    for copy in loads:
-        copy.wait()
-    for h in range(heads):
-        keys_t[h] = keys[h].T
-    acc_k[...] = jnp.zeros_like(acc_k)
-    acc_v[...] = jnp.zeros_like(acc_v)
     pl.semaphore_wait(barrier, count)
 
     def fwd_copy(c, src, dst, device):
@@ -140,7 +136,7 @@
             src_ref=mark_out.at[slot], dst_ref=mark_in.at[mirror(slot)], send_sem=mark_s.at[slot],
             recv_sem=mark_r.at[mirror(slot)], device_id=sent_to(slot), device_id_type=MESH)
 
-    def take_marks(c):
+    def take_marks():
         for slot in range(SLOTS):
             if slot != OWN:
                 when(exists(slot), lambda slot=slot: pltpu.make_async_copy(
@@ -172,6 +168,11 @@
         for a, b, device, ok in fwd_plan:
             if a == src:
                 when(ok, lambda a=a, b=b, device=device: fwd_copy(c, a, b, device).start())
+
+    def send_own(c):
+        for n in range(2):
+            pltpu.make_async_copy(fwd.at[c, OWN, n], fwd.at[c, OWN, n], load_sem.at[2 * c + n]).wait()
+        send_fwd(c, OWN)
 
     def relay(c, src):
         def go():
@@ -242,120 +243,25 @@
             low_ds[pl.ds(j * tile, tile), :] = (p * (dp[span] - delta)).astype(jnp.bfloat16)
         acc_v[h] += dot(low_p[...], g, ((1,), (0,)))
         acc_k[h] += dot(low_ds[...], q, ((1,), (0,)))
-        return dot(keys_t[h], low_ds[...], ((1,), (0,)))
-
-    def hand_back(c, slot):
-        def go():
-            for src, ok in ret_adds.get(slot, ()):
-                def add(src=src):
-                    local_wait(ret_in, ret_r, c, src)
-                    part[c % 2, slot] += ret_in[c, src].astype(jnp.float32)
-                when(ok, add)
-            if slot == OWN:
-                rows_at = pl.multiple_of((c % per_head) * chunk, chunk)
-                out_q[c // per_head, pl.ds(rows_at, chunk), :] = (part[c % 2, slot] * scale).T.astype(jnp.bfloat16)
-            else:
-                ret_out[c, slot] = part[c % 2, slot].astype(jnp.bfloat16)
-                ret_copy(c, slot, ret_device[slot]).start()
-        when(exists(slot), go)
-
-    def exists_dyn(slot):
-        a = slot % 3
-        ok = jnp.logical_or(a != 0, has_m)
-        ok = both(ok, jnp.logical_or(a != 2, has_p))
-        return both(ok, jnp.logical_or(slot // 3 != 2, has_xi))
-
-    def relay_1(c):
-        relay(c, OTHER_0)
-        relay(c, OTHER_M)
-
-    events = (
-        (SEND_OWN, lambda c: send_fwd(c, OWN)), (RELAY_1, relay_1), (RELAY_2, lambda c: relay(c, SAME_M)),
-        (RELAY_3, lambda c: relay(c, OTHER_P)), (MERGE, merge),
-        (RET_OTHER_P, lambda c: hand_back(c, OTHER_P)), (RET_OTHER_M, lambda c: hand_back(c, OTHER_M)),
-        (RET_SAME_M, lambda c: hand_back(c, SAME_M)), (RET_OTHER_0, lambda c: hand_back(c, OTHER_0)),
-        (RET_OWN, lambda c: hand_back(c, OWN)),
-    )
-
-    def place(it, b, offset):
-        late = b < offset % SLOTS
-        c = it - offset // SLOTS - late.astype(jnp.int32)
-        index = b - offset % SLOTS + jnp.where(late, SLOTS, 0)
-        return c, index, both(c >= 0, c < chunks)
-
-    for slot in range(SLOTS):
-        if slot != OWN:
-            when(exists(slot), lambda slot=slot: mark_copy(slot).start())
-
-    def step(it, b):
-        for k in range(SLOTS):
-            here = [(offset // SLOTS, fn) for offset, fn in events if offset % SLOTS == k]
-
-            def run(here=here):
-                for lag, fn in here:
-                    c = it - lag
-                    pl.when(both(c >= 0, c < chunks))(lambda fn=fn, c=c: fn(c))
-
-            if here:
-                pl.when(b == k)(run)
-
-        @pl.when(both(it == TAKE_MARKS // SLOTS, b == TAKE_MARKS % SLOTS))
+        dq_t = dot(keys_t[h], low_ds[...], ((1,), (0,)))
+        part[c % 4, slot] = dq_t
+        ret_out[c, slot] = dq_t.astype(jnp.bfloat16)
+
+    def store(h, n):
+        src, ref = ((out_q, dq_hbm), (out_k, dk_hbm), (out_v, dv_hbm))[n]
+        columns = pl.ds(h * HD if isinstance(h, int) else pl.multiple_of(h * HD, HD), HD)
+        return pltpu.make_async_copy(src.at[h], ref.at[:, columns], store_sem.at[h, n])
+
+    def store_kv(c):
+        @pl.when(c % per_head == per_head - 1)
         def _():
-            take_marks(0)
-
-        c1, i1, ok1 = place(it, b, FIRST)
-        b1 = pick(FIRST_ORDER, i1)
-
-        @pl.when(both(ok1, exists_dyn(b1)))
-        def _():
-            @pl.when(jnp.logical_or(i1 == FIRST_ORDER.index(SAME_P), i1 >= FIRST_ORDER.index(CROSS_0)))
-            def _():
-                local_wait(fwd, fwd_r, c1, b1)
-
-            first_pass(c1, b1)
-
-            @pl.when(b1 != OWN)
-            def _():
-                st_copy(c1, b1).start()
-
-        c2, i2, ok2 = place(it, b, SECOND)
-        b2 = pick(SECOND_ORDER, i2)
-
-        @pl.when(both(ok2, exists_dyn(b2)))
-        def _():
-            @pl.when(b2 != OWN)
-            def _():
-                local_wait(bc_in, bc_r, c2, b2)
-
-            term = second_pass(c2, b2)
-
-            @pl.when(i2 >= 4)
-            def _():
-                part[c2 % 2, b2] = term
-
-            @pl.when(i2 < 4)
-            def _():
-                ret_out[c2, b2] = term.astype(jnp.bfloat16)
-                ret_copy(c2, b2, {"tm": jnp.where(i2 == 3, t + s, t - 2 * s), "row": r}).start()
-
-    def chunk_steps(it, carry):
-        def one(b, carry):
-            step(it, b)
-            return carry
-        return lax.fori_loop(0, SLOTS, one, carry)
-
-    lax.fori_loop(0, chunks + RET_OWN // SLOTS, chunk_steps, 0)
-
-    out_k[...] = (acc_k[...] * scale).astype(jnp.bfloat16)
-    out_v[...] = acc_v[...].astype(jnp.bfloat16)
-    stores = []
-    for h in range(heads):
-        for src, ref in ((out_q, dq_hbm), (out_k, dk_hbm), (out_v, dv_hbm)):
-            stores.append(pltpu.make_async_copy(src.at[h], ref.at[:, pl.ds(h * HD, HD)], load_sem.at[len(stores)]))
-    for copy in stores:
-        copy.start()
-
-    def drain(c, carry):
+            h = c // per_head
+            out_k[h] = (acc_k[h] * scale).astype(jnp.bfloat16)
+            out_v[h] = acc_v[h].astype(jnp.bfloat16)
+            store(h, 1).start()
+            store(h, 2).start()
+
+    def drain(c):
         for a, b, device, ok in fwd_plan:
             when(ok, lambda a=a, b=b, device=device: fwd_copy(c, a, b, device).wait_send())
         for slot in range(SLOTS):
@@ -365,14 +271,120 @@
                     bc_copy(c, slot).wait_send()
                     ret_copy(c, slot, ret_device[slot]).wait_send()
                 when(exists(slot), go)
-        return carry
-
-    lax.fori_loop(0, chunks, drain, 0)
+
+    def hand_back(c, slot):
+        def go():
+            for src, ok in ret_adds.get(slot, ()):
+                def add(src=src):
+                    local_wait(ret_in, ret_r, c, src)
+                    part[c % 4, slot] += ret_in[c, src].astype(jnp.float32)
+                when(ok, add)
+            if slot == OWN:
+                rows_at = pl.multiple_of((c % per_head) * chunk, chunk)
+                out_q[c // per_head, pl.ds(rows_at, chunk), :] = (part[c % 4, slot] * scale).T.astype(jnp.bfloat16)
+
+                @pl.when(c % per_head == per_head - 1)
+                def _():
+                    store(c // per_head, 0).start()
+            else:
+                ret_out[c, slot] = part[c % 4, slot].astype(jnp.bfloat16)
+                ret_copy(c, slot, ret_device[slot]).start()
+        when(exists(slot), go)
+
+    def exists_dyn(slot):
+        a = slot % 3
+        ok = jnp.logical_or(a != 0, has_m)
+        ok = both(ok, jnp.logical_or(a != 2, has_p))
+        return both(ok, jnp.logical_or(slot // 3 != 2, has_xi))
+
+    def relay_1(c):
+        relay(c, OTHER_0)
+        relay(c, OTHER_M)
+
+    events = (
+        (SEND_OWN, send_own), (RELAY_1, relay_1), (RELAY_2, lambda c: relay(c, SAME_M)),
+        (RELAY_3, lambda c: relay(c, OTHER_P)), (MERGE, merge),
+        (RET_OTHER_P, lambda c: hand_back(c, OTHER_P)), (RET_OTHER_M, lambda c: hand_back(c, OTHER_M)),
+        (RET_SAME_M, lambda c: hand_back(c, SAME_M)), (RET_OTHER_0, lambda c: hand_back(c, OTHER_0)),
+        (RET_OWN, lambda c: hand_back(c, OWN)), (STORE_KV, store_kv), (DRAIN, drain),
+    )
+
+    def place(it, b, offset):
+        late = b < offset % SLOTS
+        c = it - offset // SLOTS - late.astype(jnp.int32)
+        index = b - offset % SLOTS + jnp.where(late, SLOTS, 0)
+        return c, index, both(c >= 0, c < chunks)
+
+    for slot in range(SLOTS):
+        if slot != OWN:
+            when(exists(slot), lambda slot=slot: mark_copy(slot).start())
+
+    def step(it, b):
+        for k in range(SLOTS):
+            here = [(offset // SLOTS, fn) for offset, fn in events if offset % SLOTS == k]
+
+            def run(here=here):
+                for lag, fn in here:
+                    c = it - lag
+                    pl.when(both(c >= 0, c < chunks))(lambda fn=fn, c=c: fn(c))
+
+            if here:
+                pl.when(b == k)(run)
+
+        @pl.when(both(it == SET_UP // SLOTS, b == SET_UP % SLOTS))
+        def _():
+            for copy in loads[2 * chunks:]:
+                copy.wait()
+            for h in range(heads):
+                keys_t[h] = keys[h].T
+            acc_k[...] = jnp.zeros_like(acc_k)
+            acc_v[...] = jnp.zeros_like(acc_v)
+            take_marks()
+
+        c1, i1, ok1 = place(it, b, FIRST)
+        b1 = pick(FIRST_ORDER, i1)
+
+        @pl.when(both(ok1, exists_dyn(b1)))
+        def _():
+            @pl.when(jnp.logical_or(b1 == SAME_P, b1 >= CROSS_M))
+            def _():
+                local_wait(fwd, fwd_r, c1, b1)
+
+            first_pass(c1, b1)
+
+            @pl.when(b1 != OWN)
+            def _():
+                st_copy(c1, b1).start()
+
+        c2, i2, ok2 = place(it, b, SECOND)
+        b2 = pick(SECOND_ORDER, i2)
+
+        @pl.when(both(ok2, exists_dyn(b2)))
+        def _():
+            @pl.when(b2 != OWN)
+            def _():
+                local_wait(bc_in, bc_r, c2, b2)
+
+            second_pass(c2, b2)
+
+            @pl.when(jnp.logical_or(b2 == SAME_P, b2 >= CROSS_M))
+            def _():
+                ret_copy(c2, b2, {"tm": jnp.where(b2 == SAME_P, t + s, t - 2 * s), "row": r}).start()
+
+    def chunk_steps(it, carry):
+        def one(b, carry):
+            step(it, b)
+            return carry
+        return lax.fori_loop(0, SLOTS, one, carry)
+
+    lax.fori_loop(0, chunks + DRAIN // SLOTS, chunk_steps, 0)
+
     for slot in range(SLOTS):
         if slot != OWN:
             when(exists(slot), lambda slot=slot: mark_copy(slot).wait_send())
-    for copy in stores:
-        copy.wait()
+    for h in range(heads):
+        for n in range(3):
+            store(h, n).wait()
 
 
 def per_device(times, rows, query, key_tiles, value_tiles, grad_out, neighbours):
@@ -383,7 +395,8 @@
     chunk = tokens // per_head
     chunks = heads * per_head
     entries = neighbours[0, 0]
-    place = jnp.array([3 * ((slot // 3 + 1) % 3 - 1) + slot % 3 - 1 for slot in range(SLOTS)], jnp.int32)
+    slots = jnp.arange(SLOTS, dtype=jnp.int32)
+    place = 3 * ((slots // 3 + 1) % 3 - 1) + slots % 3 - 1
     code = 4 + place * (1 - 2 * (lax.axis_index("tm") % 2))
     names = code[:, None] * count + jnp.arange(count * count, dtype=jnp.int32) % count
     listed = jnp.any(names[:, :, None] == jnp.repeat(entries, count, axis=0)[None], axis=2)
@@ -406,7 +419,7 @@
             vmem((heads, HD, tokens), jnp.bfloat16),
             vmem((heads, tokens, HD), jnp.float32),
             vmem((heads, tokens, HD), jnp.float32),
-            vmem((2, SLOTS, HD, chunk), jnp.float32),
+            vmem((4, SLOTS, HD, chunk), jnp.float32),
             vmem((chunks, SLOTS, HD, chunk), jnp.bfloat16),
             vmem((chunks, SLOTS, HD, chunk), jnp.bfloat16),
             vmem(small, jnp.float32),
@@ -422,6 +435,7 @@
             vmem((per_head, SLOTS, 2, chunk), jnp.float32),
             dma((SLOTS,)),
             dma((SLOTS,)),
+            dma((heads, 3)),
         ],
         compiler_params=pltpu.CompilerParams(
             collective_id=0, has_side_effects=True, vmem_limit_bytes=56 * 1024 * 1024

time: 170 us -> 163 us (0.959)
  Pallas kernels: 163 us -> 156 us
    pallas_call x1, Pallas kernels: 163 us -> 156 us  [per_device(): pl.pallas_call(functools.partial(kernel, times, rows, heads, tile), out_s...]
    unnamed x11 -> x9, local copies, waits for them, and re-layouts: 5.35 us -> 4.7 us
where the time goes in v3:
time: 163 us
  Pallas kernels  156 us (96%)
  local copies, waits for them, and re-layouts  5.48 us (3%)
    pallas_call x1, Pallas kernels, per_device(): pl.pallas_call(functools.partial(kernel, times, rows, heads, tile), out_s...  156 us
    unnamed x9, local copies, waits for them, and re-layouts  4.7 us

profile of v3, /device:TPU:20, one launch (start us, length us, event | category | flops | bytes accessed | tf_op | source)
XLA Modules:
  0.0 162.6 jit_solution(11501038383083387270)
XLA Ops:
  0.7 0.0 copy-start.2
  0.7 0.1 broadcast_add_fusion
  0.8 0.6 copy-done.2
  1.4 0.1 compare_reduce_fusion
  1.5 0.1 copy.8
  1.6 0.7 broadcast_in_dim.5.mark_out
  2.2 156.2 %shard_map.76 = (bf16[768,384]{1,0:T(8,128)(2,1)}, bf16[768,384]{1,0:T(8,128)(2,1)}, bf16[768,384]{1,0:T(8,128)(2,1)}) custom-call(bf16[768,384]{1,0:T(8,128)(2,1)} %bitcast.12, bf16[768,384]{1,0:T(8,128)(2,1)} %bitcast.13, bf16[768,384]{1,0:T(8,128)(2,1)} %bitcast.14, bf16[768,384]{1,0:T(8,128)(2,1)} %bitcast.15, f32[9,4,128]{2,1,0:T(4,128)} %broadcast_in_dim.5.mark_out), custom_call_target="tpu_custom_call" | custom-call | tf_op jit(solution)/shard_map/pallas_call | solution.py:410
  158.5 0.0 copy-start.1
  158.5 2.0 %copy.12 = bf16[1,1,2,384,384]{4,3,2,1,0:T(8,128)(2,1)} copy(bf16[1,1,2,384,384]{4,3,2,1,0:T(8,128)(2,1)} %bitcast.11) | data formatting | bytes 1179648
  160.5 0.0 copy-done.1
  160.5 0.0 copy-start
  160.5 0.8 copy.13
  161.3 0.5 copy-done
  161.7 0.8 copy.14
  (4 shorter events, 0.0 us)
Async XLA Ops:
  0.7 0.7 copy-start.2
  158.5 2.0 %copy-start.1 = (bf16[768,384]{1,0:T(8,128)(2,1)S(1)}, bf16[768,384]{1,0:T(8,128)(2,1)}, u32[]{:S(2)}) copy-start(bf16[768,384]{1,0:T(8,128)(2,1)} %get-tuple-element.7) | copy-start | bytes 1769476
  160.5 1.3 copy-start

commit v4 on v3

--- a/solution.py
+++ b/solution.py
@@ -302,9 +302,9 @@
         relay(c, OTHER_M)
 
     events = (
+        (RET_OTHER_P, lambda c: hand_back(c, OTHER_P)), (RET_OTHER_M, lambda c: hand_back(c, OTHER_M)),
         (SEND_OWN, send_own), (RELAY_1, relay_1), (RELAY_2, lambda c: relay(c, SAME_M)),
         (RELAY_3, lambda c: relay(c, OTHER_P)), (MERGE, merge),
-        (RET_OTHER_P, lambda c: hand_back(c, OTHER_P)), (RET_OTHER_M, lambda c: hand_back(c, OTHER_M)),
         (RET_SAME_M, lambda c: hand_back(c, SAME_M)), (RET_OTHER_0, lambda c: hand_back(c, OTHER_0)),
         (RET_OWN, lambda c: hand_back(c, OWN)), (STORE_KV, store_kv), (DRAIN, drain),
     )

time: 163 us -> 162 us (level)
  no operation moved by 1% of the time
where the time goes in v4:
time: 162 us
  Pallas kernels  155 us (96%)
  local copies, waits for them, and re-layouts  5.48 us (3%)
    pallas_call x1, Pallas kernels, per_device(): pl.pallas_call(functools.partial(kernel, times, rows, heads, tile), out_s...  155 us
    unnamed x9, local copies, waits for them, and re-layouts  4.7 us

profile of v4, /device:TPU:20, one launch (start us, length us, event | category | flops | bytes accessed | tf_op | source)
XLA Modules:
  0.0 161.7 jit_solution(5741063992103668120)
XLA Ops:
  0.7 0.0 copy-start.2
  0.7 0.1 broadcast_add_fusion
  0.8 0.6 copy-done.2
  1.4 0.1 compare_reduce_fusion
  1.5 0.1 copy.8
  1.6 0.7 broadcast_in_dim.5.mark_out
  2.2 155.3 %shard_map.76 = (bf16[768,384]{1,0:T(8,128)(2,1)}, bf16[768,384]{1,0:T(8,128)(2,1)}, bf16[768,384]{1,0:T(8,128)(2,1)}) custom-call(bf16[768,384]{1,0:T(8,128)(2,1)} %bitcast.12, bf16[768,384]{1,0:T(8,128)(2,1)} %bitcast.13, bf16[768,384]{1,0:T(8,128)(2,1)} %bitcast.14, bf16[768,384]{1,0:T(8,128)(2,1)} %bitcast.15, f32[9,4,128]{2,1,0:T(4,128)} %broadcast_in_dim.5.mark_out), custom_call_target="tpu_custom_call" | custom-call | tf_op jit(solution)/shard_map/pallas_call | solution.py:410
  157.6 0.0 copy-start.1
  157.6 2.0 %copy.12 = bf16[1,1,2,384,384]{4,3,2,1,0:T(8,128)(2,1)} copy(bf16[1,1,2,384,384]{4,3,2,1,0:T(8,128)(2,1)} %bitcast.11) | data formatting | bytes 1179648
  159.6 0.0 copy-done.1
  159.6 0.0 copy-start
  159.6 0.8 copy.13
  160.4 0.5 copy-done
  160.9 0.8 copy.14
  (4 shorter events, 0.0 us)
Async XLA Ops:
  0.7 0.7 copy-start.2
  157.6 2.0 %copy-start.1 = (bf16[768,384]{1,0:T(8,128)(2,1)S(1)}, bf16[768,384]{1,0:T(8,128)(2,1)}, u32[]{:S(2)}) copy-start(bf16[768,384]{1,0:T(8,128)(2,1)} %get-tuple-element.7) | copy-start | bytes 1769476
  159.6 1.3 copy-start
